TPU v7x, 32 devices: a whole 2x2x4 slice. The times are simulated.
32 devices in a mesh: mem: 8 (over y, x, core), cell: 4 (over z).
Axes of the slice: x: 2, y: 2, z: 4, core: 2. Of those that a mesh axis runs over, the one named last changes fastest.
Arguments:
- prior_ensemble: bfloat16 [512, 2, 32768], P('mem', None, 'cell'), may hold values from -12 to 12
- measurement_location: int32 [16, 1024], P('cell', 'mem'), may hold values from 0 to 65535, as said below
- measurement_datum: float32 [16, 1024], P('cell', 'mem'), may hold values from -32 to 32
- measurement_spread: float32 [16, 1024], P('cell', 'mem'), may hold values from 1.2 to 20
Outputs:
- analysis: bfloat16 [512, 2, 32768], P('mem', None, 'cell')
Inputs may be any that keep to these rules, and one draw needn't show every extreme that they name: `measurement_location`: with v an entry at row r and column c, v // 32768 is its field and v % 32768 its cell; that cell is one of the 1024 cells that begin at ((r // 4) * 8 + c // 128) * 1024. Within each such block of 4 rows and 128 columns the entries are distinct, and they include the first cell of field 0 and the last cell of field 1 of that range.
All inputs are finite; a program needn't handle non-finite values.
Results may differ from a plain program's by a relative error of at most 0.0063.
Values may be sent and summed in bfloat16 or wider, within the bound.
A program may use at most 64 MiB of HBM per device.

v0:
```python
import math

import jax
import jax.numpy as jnp
from jax import lax
from jax.sharding import PartitionSpec as P

NS_ITERS = 8


def local(prior_ensemble, measurement_location, measurement_datum, measurement_spread):
    highest = lax.Precision.HIGHEST
    gathered_lines = lax.all_to_all(prior_ensemble, "mem", split_axis=2, concat_axis=0, tiled=True)
    ensemble_size, fields, cell_dev = gathered_lines.shape
    norm_factor = math.sqrt(ensemble_size - 1)
    flat_state = gathered_lines.reshape(ensemble_size, fields * cell_dev)
    mean_state = jnp.sum(flat_state, axis=0, dtype=jnp.float32) / ensemble_size
    anomalies = (flat_state - mean_state).astype(jnp.bfloat16)
    grid_site_number = prior_ensemble.shape[2] * lax.axis_size("cell")
    block_start = (lax.axis_index("cell") * lax.axis_size("mem") + lax.axis_index("mem")) * cell_dev
    cell_ids = measurement_location.reshape(-1)
    local_slots = cell_ids // grid_site_number * cell_dev + (
        cell_ids % grid_site_number - block_start
    )
    errors = measurement_spread.reshape(-1)
    picked_lines = jnp.take(anomalies, local_slots, axis=1)
    scaled = (picked_lines.astype(jnp.float32) / (errors * norm_factor)).astype(jnp.bfloat16)
    innovation = (
        (measurement_datum.reshape(-1) - jnp.take(mean_state, local_slots)) / errors
    ).astype(jnp.bfloat16)
    gram_part = lax.dot_general(
        scaled, scaled, (((1,), (1,)), ((), ())), preferred_element_type=jnp.float32
    )
    proj_part = jnp.dot(
        scaled.astype(jnp.float32), innovation.astype(jnp.float32), precision=highest
    )
    row_count = ensemble_size // lax.axis_size("mem")
    row_start = lax.axis_index("mem") * row_count
    identity = jnp.eye(ensemble_size, dtype=jnp.float32)
    gram_sum, projected = lax.psum((gram_part, proj_part), ("mem", "cell"))
    system = gram_sum + identity
    norm_scale = jnp.sqrt(jnp.sum(system * system))

    def whole_turn(turn, pair):
        whole_y, whole_z = pair
        newton_step = 1.5 * identity - 0.5 * jnp.dot(whole_z, whole_y, precision=highest)
        return (
            jnp.dot(newton_step, whole_y, precision=highest),
            jnp.dot(newton_step, whole_z, precision=highest),
        )

    whole_y, whole_z = lax.fori_loop(0, NS_ITERS, whole_turn, (system / norm_scale, identity))
    iterate_z = lax.dynamic_slice_in_dim(whole_z, row_start, row_count, 0)
    divisor = jnp.sqrt(norm_scale) * norm_factor
    shift_part = jnp.dot(iterate_z, projected, precision=highest)
    shift_weights = lax.all_gather(shift_part, "mem", axis=0, tiled=True) / divisor
    weight_rows = (iterate_z / jnp.sqrt(norm_scale)).astype(jnp.bfloat16)
    updated = jnp.dot(
        lax.all_gather(weight_rows, "mem", axis=0, tiled=True),
        anomalies,
        preferred_element_type=jnp.float32,
    )
    mean_shift = jnp.dot(shift_weights, updated, precision=highest)
    analysis = (
        (mean_state + mean_shift + updated)
        .astype(jnp.bfloat16)
        .reshape(ensemble_size, fields, cell_dev)
    )
    return lax.all_to_all(analysis, "mem", split_axis=0, concat_axis=2, tiled=True)


def solution(mesh):
    placed = (P("mem", None, "cell"), P("cell", "mem"), P("cell", "mem"), P("cell", "mem"))
    return jax.shard_map(
        local, mesh=mesh, in_specs=placed, out_specs=P("mem", None, "cell"), check_vma=False
    )
```

profile of v0, /device:TPU:0, one launch (start us, length us, event | category | flops | bytes accessed | tf_op | source)
XLA Modules:
  0.0 372.0 jit_solution(4964061703157303378)
XLA Ops:
  6.5 11.4 %copy.30 = bf16[64,2,8192]{0,1,2:T(2,128)(2,1)} copy(bf16[64,2,8192]{2,1,0:T(2,128)(2,1)} %param.6) | data formatting | bytes 4194304 | tf_op args[0]
  17.9 7.6 %reshape.190 = bf16[8,2,65536]{2,1,0:T(2,128)(2,1)} reshape(bf16[8192,2,64]{2,1,0:T(2,128)(2,1)} %bitcast.93) | data formatting | bytes 4194304
  25.5 5.2 %all-to-all-start = ((bf16[8,2,65536]{2,1,0:T(2,128)(2,1)}), bf16[8,2,65536]{2,1,0:T(2,128)(2,1)S(1)}, u32[]{:S(2)}, u32[]{:S(2)}) async-start(bf16[8,2,65536]{2,1,0:T(2,128)(2,1)} %reshape.190), calls=%async_computation | async-start | bytes 4194304 | tf_op jit(solution)/shard_map/all_to_all | solution.py:13
  30.8 26.5 %all-to-all-done = bf16[8,2,65536]{2,1,0:T(2,128)(2,1)S(1)} async-done(((bf16[8,2,65536]{2,1,0:T(2,128)(2,1)}), bf16[8,2,65536]{2,1,0:T(2,128)(2,1)S(1)}, u32[]{:S(2)}, u32[]{:S(2)}) %all-to-all-start) | async-done | bytes 2097184 | tf_op jit(solution)/shard_map/all_to_all | solution.py:13
  57.3 5.0 %reshape.191 = bf16[8192,2,64]{2,1,0:T(2,128)(2,1)} reshape(bf16[8,2,65536]{2,1,0:T(2,128)(2,1)S(1)} %all-to-all-done) | data formatting | bytes 4194304
  62.3 16.8 %convert_reduce_fusion = f32[2,8192]{0,1:T(8,128)} fusion(bf16[8192,2,64]{2,1,0:T(2,128)(2,1)} %reshape.191), kind=kLoop, calls=%fused_computation.9 | loop fusion | flops 2080768 | bytes 2162688 | tf_op jit(solution)/shard_map/reduce_sum | solution.py:17
  79.1 2.5 reduce_sum.27
  81.7 0.2 copy.39
  81.9 11.4 %copy.33 = f32[64,2,8,1024]{3,1,0,2:T(2,128)} copy(bf16[64,2,8,1024]{0,1,3,2:T(2,128)(2,1)} %bitcast.92) | data formatting | bytes 6291456 | tf_op jit(solution)/shard_map/convert_element_type | solution.py:17
  93.3 6.1 %copy.38 = f32[64,8,2,1024]{3,1,2,0:T(8,128)} copy(f32[64,8,2,1024]{3,2,1,0:T(2,128)} %bitcast.94) | data formatting | bytes 8388608
  99.4 5.3 %copy.34 = f32[512,2048]{0,1:T(8,128)} copy(f32[512,2048]{1,0:T(8,128)} %bitcast.95) | data formatting | bytes 8388608 | tf_op jit(solution)/shard_map/convert_element_type | solution.py:17
  104.7 3.1 gather_fusion.1
  107.9 2.5 subtract_convert_fusion
  110.5 2.0 gather_fusion
  112.5 0.2 divide_convert_fusion
  112.7 1.5 fusion.22
  114.3 0.6 dynamic-slice
  115.5 0.1 fusion.3
  115.6 0.2 fusion.4
  115.8 39.7 %psum.15 = f32[512]{0:T(512)S(1)} all-reduce(f32[512]{0:T(512)S(1)} %bitcast.103), channel_id=1, replica_groups=mesh['mem'=8,'cell'=4] {'mem','cell'}, use_global_device_ids=true, to_apply=%region_6.7 | all-reduce | flops 512 | bytes 4096 | tf_op jit(solution)/shard_map/psum | solution.py:40
  155.5 88.4 %all-reduce.3.cloned.1.call-done = f32[512,512]{1,0:T(8,128)} async-done(((f32[512,512]{1,0:T(8,128)}), f32[512,512]{1,0:T(8,128)}) %all-reduce.3.cloned.1.call-update) | async-done | bytes 1048592 | tf_op jit(solution)/shard_map/psum | solution.py:40
  243.9 2.2 multiply_reduce_fusion
  246.9 1.4 broadcast_divide_fusion
  248.2 45.9 %while.13 = (s32[]{:T(128)}, f32[512,512]{1,0:T(8,128)S(1)}, f32[512,512]{1,0:T(8,128)S(1)}, s32[]{:T(128)}) while((s32[]{:T(128)}, f32[512,512]{1,0:T(8,128)S(1)}, f32[512,512]{1,0:T(8,128)S(1)}, s32[]{:T(128)}) %tuple.23), condition=%wide.region_5.6_spmd.clone, body=%wide.region_4.5_spmd.clone.sunk | while | flops 4832886784 | bytes 13631541 | solution.py:52
  248.3 0.1 copy.61
  248.3 0.1 copy.60
  248.4 1.8 fusion.54
  250.3 1.8 fusion.55
  252.1 1.8 fusion.56
  254.0 0.1 copy.61
  254.1 0.1 copy.60
  254.2 1.9 fusion.54
  256.0 1.8 fusion.55
  257.9 1.8 fusion.56
  259.7 0.1 copy.61
  259.9 1.8 fusion.54
  261.7 1.8 fusion.55
  263.6 1.8 fusion.56
  265.6 1.9 fusion.54
  267.5 1.8 fusion.55
  269.3 1.8 fusion.56
  271.4 1.9 fusion.54
  273.2 1.8 fusion.55
  275.1 1.8 fusion.56
  277.1 1.8 fusion.54
  279.0 1.8 fusion.55
  280.8 1.8 fusion.56
  282.8 1.9 fusion.54
  284.7 1.8 fusion.55
  286.6 1.8 fusion.56
  288.6 1.8 fusion.54
  290.4 1.8 fusion.55
  292.3 1.8 fusion.56
  294.2 9.8 %all_gather.7 = bf16[512,512]{1,0:T(8,128)(2,1)S(1)} all-gather(bf16[64,512]{1,0:T(8,128)(2,1)S(1)} %divide_convert_fusion.1), channel_id=1, replica_groups=mesh['mem'=8,'cell'=4] {'mem'}, dimensions={0}, use_global_device_ids=true | all-gather | bytes 589824 | tf_op jit(solution)/shard_map/all_gather | solution.py:59
  304.0 4.8 %fusion.23 = f32[512,2048]{1,0:T(8,128)} fusion(bf16[512,512]{1,0:T(8,128)(2,1)S(1)} %all_gather.7, bf16[512,2048]{0,1:T(8,128)(2,1)} %copy-done.1), kind=kOutput, calls=%fused_computation.57 | convolution fusion | flops 1073741824 | bytes 6815744 | tf_op jit(solution)/shard_map/dot_general | solution.py:58
  308.8 0.2 convolution_bitcast_fusion
  309.0 0.2 dynamic-update-slice
  309.2 13.2 %all-reduce = f32[512]{0:T(512)S(1)} all-reduce(f32[512]{0:T(512)S(1)} %dynamic-update-slice), channel_id=1, replica_groups=mesh['mem'=8,'cell'=4] {'mem'}, use_global_device_ids=true, to_apply=%add | all-reduce | flops 512 | bytes 4096
  322.4 4.4 %fusion.24 = f32[1,2048]{1,0:T(1,128)S(1)} fusion(f32[512,1]{0,1:T(1,128)S(1)} %bitcast.104, f32[512,2048]{1,0:T(8,128)} %fusion.23), kind=kOutput, calls=%fused_computation.58 | convolution fusion | flops 12582912 | bytes 4204544 | tf_op jit(solution)/shard_map/dot_general | solution.py:63
  326.8 0.5 add_convert_fusion
  327.3 2.8 reshape.160
  330.1 30.1 %all_to_all.27 = bf16[512,2,1024]{2,1,0:T(2,128)(2,1)S(1)} all-to-all(bf16[512,2,1024]{2,1,0:T(2,128)(2,1)} %reshape.160), channel_id=1, replica_groups=mesh['mem'=8,'cell'=4] {'mem'}, dimensions={0} | all-to-all | bytes 4194304 | tf_op jit(solution)/shard_map/all_to_all | solution.py:69
  360.2 2.2 copy.44
  362.4 2.8 all_to_all.24
  (35 shorter events, 1.0 us)
Async XLA Ops:
  17.9 12.8 %copy-start.2 = (s32[4,128]{1,0:T(4,128)S(1)}, s32[4,128]{1,0:T(4,128)}, u32[]{:S(2)}) copy-start(s32[4,128]{1,0:T(4,128)} %param.7) | copy-start | bytes 6148
  25.5 31.8 %all-to-all-start = ((bf16[8,2,65536]{2,1,0:T(2,128)(2,1)}), bf16[8,2,65536]{2,1,0:T(2,128)(2,1)S(1)}, u32[]{:S(2)}, u32[]{:S(2)}) async-start(bf16[8,2,65536]{2,1,0:T(2,128)(2,1)} %reshape.190), calls=%async_computation | async-start | bytes 4194304 | tf_op jit(solution)/shard_map/all_to_all | solution.py:13
  30.7 213.3 %all-reduce.3.cloned.1.call-start = ((), (), s32[]{:S(2)}) async-start(), calls=%async_computation.2 | async-start | bytes 2097152 | tf_op jit(solution)/shard_map/psum | solution.py:40
  107.9 4.6 %copy-start.3 = (f32[4,128]{1,0:T(4,128)S(1)}, f32[4,128]{1,0:T(4,128)}, u32[]{:S(2)}) copy-start(f32[4,128]{1,0:T(4,128)} %param.9) | copy-start | bytes 6148
  107.9 4.6 %copy-start.4 = (f32[4,128]{1,0:T(4,128)S(1)}, f32[4,128]{1,0:T(4,128)}, u32[]{:S(2)}) copy-start(f32[4,128]{1,0:T(4,128)} %param.8) | copy-start | bytes 6148
  110.4 3.8 %copy-start.1 = (bf16[512,2048]{0,1:T(8,128)(2,1)}, bf16[512,2048]{0,1:T(8,128)(2,1)S(1)}, u32[]{:S(2)}) copy-start(bf16[512,2048]{0,1:T(8,128)(2,1)S(1)} %subtract_convert_fusion) | copy-start | bytes 6291460
  110.5 3.8 %copy-start.5 = (u32[32]{0:T(128)S(1)}, u32[32]{0:T(128)}, u32[]{:S(2)}) copy-start(u32[32]{0:T(128)} %constant.95) | copy-start | bytes 388
  322.4 4.4 %copy-start = (f32[512,2048]{1,0:T(8,128)S(1)}, f32[512,2048]{1,0:T(8,128)}, u32[]{:S(2)}) copy-start(f32[512,2048]{1,0:T(8,128)} %fusion.23) | copy-start | bytes 12582916
Sparse Core Ops, SparseCore 0:
  114.4 129.5 all-reduce.2
where the time goes:
time: 373 us; the launch traced here: 372 us
  waiting for transfers between devices  115 us (31%)
  blocking collectives  92.9 us (25%)
  local copies, waits for them, and re-layouts  61.8 us (17%)
  matrix products  55.4 us (15%)
  other arithmetic  26.3 us (7%)
  between operations  15 us (4%)
  starting transfers between devices  5.21 us (1%)
    psum x1, waiting for transfers between devices, local(): gram_sum, projected = lax.psum((gram_part, proj_part), ('mem', 'cell'))  88.4 us
    psum x1, blocking collectives, local(): gram_sum, projected = lax.psum((gram_part, proj_part), ('mem', 'cell'))  39.7 us
    unnamed x21, local copies, waits for them, and re-layouts  31.1 us
    all_to_all x1, blocking collectives, local(): lax.all_to_all(analysis, 'mem', split_axis=0, concat_axis=2, tiled=True)  30.1 us
    all_to_all x1, waiting for transfers between devices, local(): lax.all_to_all(prior_ensemble, 'mem', split_axis=2, concat_axis=0, tiled=...  26.5 us
    reduce_sum x2, other arithmetic, local(): mean_state = jnp.sum(flat_state, axis=0, dtype=jnp.float32) / ensemble_size  19.3 us
    convert_element_type x2, local copies, waits for them, and re-layouts, local(): mean_state = jnp.sum(flat_state, axis=0, dtype=jnp.float32) / ensemble_size  16.8 us
    dot_general x8, matrix products, whole_turn(): jnp.dot(whole_z, whole_y, precision=highest)  14.8 us
  transfers between devices with their start and end apart: 2, of which 2 were waited for; matrix products, arithmetic and copies ran while one was open for 0% of the time, Pallas kernels for 0%

commit v1 on v0

v1 whole, which is shorter than its diff:
```python
import functools
import math

import jax
import jax.numpy as jnp
from jax import lax
from jax.experimental import pallas as pl
from jax.experimental.pallas import tpu as pltpu
from jax.sharding import PartitionSpec as P

NS_ITERS = 8
LANES = 128
BF, F32 = jnp.bfloat16, jnp.float32
MESH = pl.DeviceIdType.MESH


def iota(shape, dim):
    return lax.broadcasted_iota(jnp.int32, shape, dim)


def remote(src, dst, send, recv, where):
    return pltpu.make_async_remote_copy(
        src_ref=src, dst_ref=dst, send_sem=send, recv_sem=recv, device_id=where, device_id_type=MESH
    )


def nt(a, b):
    return lax.dot_general(a, b, (((1,), (1,)), ((), ())), preferred_element_type=F32)


def nn(a, b):
    return jnp.dot(a, b, preferred_element_type=F32)


def thirds(v):
    hi = v.astype(BF)
    rest = v - hi.astype(F32)
    mid = rest.astype(BF)
    lo = (rest - mid.astype(F32)).astype(BF)
    return hi, mid, lo


def row_times(v, mat):
    parts = thirds(v)
    row = iota((16, v.shape[1]), 0)
    stack = jnp.zeros((16, v.shape[1]), F32)
    for i, part in enumerate(parts):
        stack = jnp.where(row == i, part.astype(F32), stack)
    return jnp.sum(nn(stack.astype(BF), mat), axis=0, keepdims=True)


def kernel(
    dims, x, loc, datum, spread, y,
    held, anom, means, hot, scaled, gram, r1, s1, r2, s2, r3, full,
    sys_f, u_f, z_f, his, los, wts, base, outs,
    a_send, a_recv, own_sem, c_send, c_recv, q_send, q_recv, z_send, z_recv,
    zg_send, zg_recv, qg_send, qg_recv, cg_send, cg_recv, o_send, o_recv,
):
    n, nz, members, fields, cells, mloc, grid_cells = dims
    rows = mloc * fields
    nq = n // 2
    total = gram.shape[0]
    half, quart = total // 2, total // 2 // nq
    piece = quart // nz
    norm_factor = math.sqrt(members - 1)
    me, mz = lax.axis_index("mem"), lax.axis_index("cell")
    core, chip = lax.rem(me, 2), lax.div(me, 2)
    mate = me + 1 - 2 * core

    barrier = pltpu.get_barrier_semaphore()
    for d in range(1, n):
        pl.semaphore_signal(barrier, inc=1, device_id={"mem": lax.rem(me + d, n)}, device_id_type=MESH)
    for d in range(1, nz):
        pl.semaphore_signal(barrier, inc=1, device_id={"cell": lax.rem(mz + d, nz)}, device_id_type=MESH)
    pl.semaphore_wait(barrier, n - 1 + nz - 1)

    def col(p):
        return pl.ds(pl.multiple_of(p * cells, cells), cells)

    def block(p):
        return pl.ds(pl.multiple_of(p * rows, rows), rows)

    def share(p):
        return pl.ds(pl.multiple_of(p * mloc, mloc), mloc)

    def send_in(d, _):
        p = lax.rem(me + d, n)
        remote(x.at[:, col(p)], held.at[block(me)], a_send.at[d], a_recv.at[d], {"mem": p}).start()
        return 0

    lax.fori_loop(1, n, send_in, 0)
    own = pltpu.make_async_copy(x.at[:, col(me)], held.at[block(me)], own_sem)
    own.start()

    first_cell = (mz * n + me) * cells
    obs_rows = loc.shape[0]
    obs = obs_rows * LANES
    v = loc[...]
    slots = v - first_cell
    for f in range(1, fields):
        slots = slots + jnp.where(v >= f * grid_cells, cells - grid_cells, 0)

    def build(i, _):
        at = pl.ds(pl.multiple_of(i * LANES, LANES), LANES)
        cell = iota((LANES, LANES), 0) + i * LANES
        for r in range(obs_rows):
            hot[at, r * LANES:(r + 1) * LANES] = jnp.where(cell == slots[r:r + 1, :], 1.0, 0.0).astype(BF)
        return 0

    lax.fori_loop(0, fields * cells // LANES, build, 0)

    means[...] = jnp.zeros_like(means)

    def take(p):
        got = held[block(p), :]
        for f in range(fields):
            pick = jnp.where(iota((mloc, rows), 1) == iota((mloc, rows), 0) * fields + f, 1.0, 0.0).astype(BF)
            lines = nn(pick, got)
            at = slice(f * cells, (f + 1) * cells)
            anom[share(p), at] = lines.astype(BF)
            means[:, at] += jnp.sum(lines, axis=0, keepdims=True)

    own.wait()
    take(me)

    def arrive(d, _):
        p = lax.rem(me + n - d, n)
        remote(x.at[:, col(p)], held.at[block(p)], a_send.at[d], a_recv.at[d], {"mem": p}).wait_recv()
        take(p)
        return 0

    lax.fori_loop(1, n, arrive, 0)
    means[...] = means[...] / members

    def centre(i, _):
        at = pl.ds(pl.multiple_of(i * 64, 64), 64)
        lines = (anom[at, :].astype(F32) - means[...]).astype(BF)
        anom[at, :] = lines
        return 0

    lax.fori_loop(0, members // 64, centre, 0)

    errors = jnp.concatenate([spread[r:r + 1, :] for r in range(obs_rows)], axis=1)
    values = jnp.concatenate([datum[r:r + 1, :] for r in range(obs_rows)], axis=1)
    inverse = 1.0 / (errors * norm_factor)
    mean_obs = row_times(means[...], hot[...])
    innovation = ((values - mean_obs) / errors).astype(BF)

    def pick_rows(i, _):
        at = pl.ds(pl.multiple_of(i * 256, 256), 256)
        scaled[at, :] = (nn(anom[at, :], hot[...]) * inverse).astype(BF)
        return 0

    lax.fori_loop(0, members // 256, pick_rows, 0)
    spread16 = jnp.where(iota((16, obs), 0) == 0, innovation.astype(F32), 0.0).astype(BF)
    projected = jnp.sum(nt(spread16, scaled[...]), axis=0, keepdims=True)

    nb = members // LANES
    lane, line = iota((LANES, LANES), 1), iota((LANES, LANES), 0)
    place = 0
    for bi in range(nb):
        strip = nt(scaled[bi * LANES:(bi + 1) * LANES, :], scaled[bi * LANES:, :])
        for bj in range(bi, nb):
            blk = strip[:, (bj - bi) * LANES:(bj - bi + 1) * LANES]
            if bi == bj:
                chunk = projected[:, bi * LANES:(bi + 1) * LANES]
                turned = pltpu.roll(jnp.broadcast_to(chunk, (8, LANES)), LANES // 2, 1)[0:1, :]
                low = lane < LANES // 2
                blk = jnp.where(low & (line == LANES - 1), chunk, blk)
                blk = jnp.where(low & (line == LANES - 2), turned, blk)
            gram[place * LANES:(place + 1) * LANES, :] = blk
            place += 1
    if place * LANES < total:
        gram[place * LANES:, :] = jnp.zeros((total - place * LANES, LANES), F32)

    def cut(start, size):
        return pl.ds(pl.multiple_of(start, 8), size)

    go = remote(gram.at[cut((1 - core) * half, half)], r1, c_send, c_recv, {"mem": mate})
    go.start()
    go.wait_recv()
    s1[...] = gram[cut(core * half, half), :] + r1[...]

    def to_chip(d):
        return lax.rem(lax.rem(chip + d, nq) * 2 + core, n)

    def plane(d):
        q = lax.rem(chip + d, nq)
        return remote(s1.at[cut(q * quart, quart)], r2.at[d], q_send.at[d], q_recv.at[d], {"mem": to_chip(d)})

    for d in range(1, nq):
        plane(d).start()
    acc = s1[cut(chip * quart, quart), :]
    for d in range(1, nq):
        plane(d).wait_recv()
        acc = acc + r2[d]
    s2[...] = acc

    def line_of(d):
        k = lax.rem(mz + d, nz)
        return remote(s2.at[cut(k * piece, piece)], r3.at[d], z_send.at[d], z_recv.at[d], {"cell": k})

    for d in range(1, nz):
        line_of(d).start()
    acc = s2[cut(mz * piece, piece), :]
    for d in range(1, nz):
        line_of(d).wait_recv()
        acc = acc + r3[d]
    mine = core * half + chip * quart
    full[cut(mine + mz * piece, piece), :] = acc

    def line_back(d, k):
        at = full.at[cut(mine + k * piece, piece)]
        return remote(at, at, zg_send.at[d], zg_recv.at[d], {"cell": lax.rem(mz + d, nz)})

    for d in range(1, nz):
        line_back(d, mz).start()
    for d in range(1, nz):
        line_back(d, lax.rem(mz + nz - d, nz)).wait_recv()

    def plane_back(d, q):
        at = full.at[cut(core * half + q * quart, quart)]
        return remote(at, at, qg_send.at[d], qg_recv.at[d], {"mem": to_chip(d)})

    def pair_back(d, c, q):
        at = full.at[cut(c * half + q * quart, quart)]
        return remote(at, at, cg_send.at[d], cg_recv.at[d], {"mem": mate})

    for d in range(1, nq):
        plane_back(d, chip).start()
    pair_back(0, core, chip).start()
    for d in range(1, nq):
        q = lax.rem(chip + nq - d, nq)
        plane_back(d, q).wait_recv()
        pair_back(d, core, q).start()
    for d in range(nq):
        pair_back(d, 1 - core, lax.rem(chip + nq - d, nq)).wait_recv()

    place = 0
    squares = jnp.zeros((1, LANES), F32)
    proj = []
    for bi in range(nb):
        for bj in range(bi, nb):
            blk = full[place * LANES:(place + 1) * LANES, :]
            place += 1
            here, there = slice(bi * LANES, (bi + 1) * LANES), slice(bj * LANES, (bj + 1) * LANES)
            if bi == bj:
                first, second = blk[LANES - 1:, :], blk[LANES - 2:LANES - 1, :]
                second = pltpu.roll(jnp.broadcast_to(second, (8, LANES)), LANES // 2, 1)[0:1, :]
                proj.append(jnp.where(iota((1, LANES), 1) < LANES // 2, first, second))
                blk = jnp.where(lane >= line, blk, blk.T) + jnp.where(lane == line, 1.0, 0.0)
                sys_f[here, here] = blk
                squares = squares + jnp.sum(blk * blk, axis=0, keepdims=True)
            else:
                sys_f[here, there] = blk
                sys_f[there, here] = blk.T
                squares = squares + 2.0 * jnp.sum(blk * blk, axis=0, keepdims=True)
    projected = jnp.concatenate(proj, axis=1)
    norm_scale = jnp.sqrt(jnp.sum(squares, axis=1, keepdims=True))
    inv_norm = 1.0 / norm_scale

    IP, IU, IQ, IT, IZ = range(5)
    step = 256 if members % 256 == 0 else LANES
    chunks = members // step

    def keep(slot, at, val):
        hi = val.astype(BF)
        his[slot, at, :] = hi
        los[slot, at, :] = (val - hi.astype(F32)).astype(BF)

    def times(a, b, finish):
        def go(i, _):
            at = pl.ds(pl.multiple_of(i * step, step), step)
            ah, al = his[a, at, :], los[a, at, :]
            finish(at, i, nn(ah, his[b]) + nn(ah, los[b]) + nn(al, his[b]))
            return 0

        lax.fori_loop(0, chunks, go, 0)

    def scale(i, _):
        at = pl.ds(pl.multiple_of(i * 64, 64), 64)
        val = sys_f[at, :] * inv_norm
        sys_f[at, :] = val
        keep(IP, at, val)
        return 0

    lax.fori_loop(0, members // 64, scale, 0)

    def quartic(into):
        def first(at, i, val):
            val = val - 4.5 * sys_f[at, :]
            u_f[at, :] = val
            keep(IU, at, val)

        times(IP, IP, first)

        def second(at, i, val):
            val = 0.0625 * val + 0.421875 * u_f[at, :] - 0.5390625 * sys_f[at, :]
            diagonal = iota((step, members), 1) == iota((step, members), 0) + i * step
            val = val + jnp.where(diagonal, 2.25, 0.0)
            for slot in into:
                keep(slot, at, val)

        times(IU, IU, second)

    def renew():
        times(IQ, IP, lambda at, i, val: keep(IT, at, val))

        def last(at, i, val):
            sys_f[at, :] = val
            keep(IP, at, val)

        times(IQ, IT, last)

    quartic((IQ, IZ))
    renew()

    def pair_turn(turn, _):
        now = IZ + turn
        quartic((IQ,))
        times(IQ, now, lambda at, i, val: keep(now + 1, at, val))
        renew()
        return 0

    lax.fori_loop(0, NS_ITERS // 2 - 2, pair_turn, 0)
    quartic((IQ,))

    def final(at, i, val):
        z_f[at, :] = val

    times(IQ, IZ + NS_ITERS // 2 - 2, final)

    root = 1.0 / jnp.sqrt(norm_scale)

    def weigh(i, carry):
        at = pl.ds(pl.multiple_of(i * 64, 64), 64)
        val = z_f[at, :]
        w = (val * root).astype(BF)
        wts[at, :] = w
        shift = jnp.sum(val * projected, axis=1, keepdims=True) * (root * (1.0 / norm_factor))
        return carry + jnp.sum(shift * w.astype(F32), axis=0, keepdims=True)

    mixed = lax.fori_loop(0, members // 64, weigh, jnp.zeros((1, members), F32))
    base[...] = means[...] + row_times(mixed, anom[...])

    def make(p):
        double = jnp.where(
            (iota((rows, mloc), 0) >= iota((rows, mloc), 1) * fields)
            & (iota((rows, mloc), 0) < iota((rows, mloc), 1) * fields + fields), 1.0, 0.0).astype(BF)
        w2 = nn(double, wts[share(p), :]).astype(BF)
        field = iota((rows, cells), 0) & (fields - 1)
        out = None
        for f in range(fields):
            at = slice(f * cells, (f + 1) * cells)
            part = nn(w2, anom[:, at]) + base[:, at]
            out = part if out is None else jnp.where(field == f, part, out)
        return out.astype(BF)

    def out_copy(d, p, to):
        return remote(outs.at[p], y.at[:, col(to)], o_send.at[d], o_recv.at[d], {"mem": p})

    def send_out(d, _):
        p = lax.rem(me + d, n)
        outs[p] = make(p)
        out_copy(d, p, me).start()
        return 0

    lax.fori_loop(1, n, send_out, 0)
    outs[me] = make(me)
    own = pltpu.make_async_copy(outs.at[me], y.at[:, col(me)], own_sem)
    own.start()

    def finish_out(d, _):
        p = lax.rem(me + n - d, n)
        out_copy(d, p, p).wait_recv()
        return 0

    lax.fori_loop(1, n, finish_out, 0)
    own.wait()

    def sent(d, _):
        p = lax.rem(me + d, n)
        remote(x.at[:, col(p)], held.at[block(me)], a_send.at[d], a_recv.at[d], {"mem": p}).wait_send()
        out_copy(d, p, me).wait_send()
        return 0

    lax.fori_loop(1, n, sent, 0)
    go.wait_send()
    for d in range(1, nq):
        plane(d).wait_send()
        plane_back(d, chip).wait_send()
    for d in range(1, nz):
        line_of(d).wait_send()
        line_back(d, mz).wait_send()
    for d in range(nq):
        pair_back(d, core, lax.rem(chip + nq - d, nq)).wait_send()


def local(prior_ensemble, measurement_location, measurement_datum, measurement_spread):
    n, nz = lax.axis_size("mem"), lax.axis_size("cell")
    mloc, fields, width = prior_ensemble.shape
    members, cells, rows = mloc * n, width // n, mloc * fields
    obs = measurement_location.size
    nb = members // LANES
    unit = 8 * n * nz
    total = -(-(nb * (nb + 1) // 2 * LANES) // unit) * unit
    half, nq = total // 2, n // 2
    quart = half // nq
    piece = quart // nz
    dims = (n, nz, members, fields, cells, mloc, width * nz)
    zslots = 4 + NS_ITERS // 2 - 1
    vm, dma = pltpu.VMEM, pltpu.SemaphoreType.DMA
    square = (members, members)
    scratch = [
        vm((n * rows, cells), BF), vm((members, fields * cells), BF), vm((1, fields * cells), F32),
        vm((fields * cells, obs), BF), vm((members, obs), BF),
        vm((total, LANES), F32), vm((half, LANES), F32), vm((half, LANES), F32),
        vm((nq, quart, LANES), F32), vm((quart, LANES), F32), vm((nz, piece, LANES), F32),
        vm((total, LANES), F32),
        vm(square, F32), vm(square, F32), vm(square, F32),
        vm((zslots,) + square, BF), vm((zslots,) + square, BF), vm(square, BF),
        vm((1, fields * cells), F32), vm((n, rows, cells), BF),
        dma((n,)), dma((n,)), dma, dma, dma, dma((nq,)), dma((nq,)), dma((nz,)), dma((nz,)),
        dma((nz,)), dma((nz,)), dma((nq,)), dma((nq,)), dma((nq,)), dma((nq,)), dma((n,)), dma((n,)),
    ]
    out = pl.pallas_call(
        functools.partial(kernel, dims),
        out_shape=jax.ShapeDtypeStruct((rows, width), BF),
        in_specs=[pl.BlockSpec(memory_space=pl.ANY)] + [pl.BlockSpec(memory_space=pltpu.VMEM)] * 3,
        out_specs=pl.BlockSpec(memory_space=pl.ANY),
        scratch_shapes=scratch,
        compiler_params=pltpu.CompilerParams(
            collective_id=0, has_side_effects=True, vmem_limit_bytes=50 * 1024 * 1024
        ),
    )(prior_ensemble.reshape(rows, width), measurement_location, measurement_datum, measurement_spread)
    return out.reshape(mloc, fields, width)


def solution(mesh):
    placed = (P("mem", None, "cell"), P("cell", "mem"), P("cell", "mem"), P("cell", "mem"))
    return jax.shard_map(
        local, mesh=mesh, in_specs=placed, out_specs=P("mem", None, "cell"), check_vma=False
    )
```

time: 373 us -> 108 us (0.29)
  waiting for transfers between devices: 115 us -> 0 us
  Pallas kernels: 0 us -> 99.7 us
  blocking collectives: 92.9 us -> 0 us
  matrix products: 55.4 us -> 0 us
  local copies, waits for them, and re-layouts: 61.8 us -> 6.78 us
  other arithmetic: 26.3 us -> 0 us
  between operations: 15 us -> 0.02 us
  starting transfers between devices: 5.21 us -> 0 us
    pallas_call x0 -> x1, Pallas kernels: none -> 99.7 us  [local(): pl.pallas_call(functools.partial(kernel, dims), out_shape=jax.ShapeDtypeS...]
    psum x1 -> x0, waiting for transfers between devices: 88.4 us -> none  [local(): gram_sum, projected = lax.psum((gram_part, proj_part), ('mem', 'cell'))]
    dot_general x29 -> x0, matrix products: 55.4 us -> none  [the longest x8 14.8 us: whole_turn(): jnp.dot(whole_z, whole_y, precision=highest)]
    psum x1 -> x0, blocking collectives: 39.7 us -> none  [local(): gram_sum, projected = lax.psum((gram_part, proj_part), ('mem', 'cell'))]
    unnamed x21 -> x6, local copies, waits for them, and re-layouts: 31.1 us -> 0.01 us
    all_to_all x1 -> x0, blocking collectives: 30.1 us -> none  [local(): lax.all_to_all(analysis, 'mem', split_axis=0, concat_axis=2, tiled=True)]
    all_to_all x1 -> x0, waiting for transfers between devices: 26.5 us -> none  [local(): lax.all_to_all(prior_ensemble, 'mem', split_axis=2, concat_axis=0, tiled=...]
    reduce_sum x3 -> x0, other arithmetic: 21.5 us -> none  [the longest x2 19.3 us: local(): mean_state = jnp.sum(flat_state, axis=0, dtype=jnp.float32) / ensemble_size]
  transfers between devices with their start and end apart: 2 -> 0, of which waited for: 2 -> 0; matrix products, arithmetic and copies ran while one was open for 0% -> 0% of each run, Pallas kernels for 0% -> 0%
where the time goes in v1:
time: 108 us; the launch traced here: 107 us
  Pallas kernels  99.7 us (92%)
  local copies, waits for them, and re-layouts  6.78 us (6%)
    pallas_call x1, Pallas kernels, local(): pl.pallas_call(functools.partial(kernel, dims), out_shape=jax.ShapeDtypeS...  99.7 us
    reshape x1, local copies, waits for them, and re-layouts, local(): prior_ensemble.reshape(rows, width)  4.14 us
    reshape x1, local copies, waits for them, and re-layouts, local(): return out.reshape(mloc, fields, width)  2.63 us

profile of v1, /device:TPU:0, one launch (start us, length us, event | category | flops | bytes accessed | tf_op | source)
XLA Modules:
  0.0 106.5 jit_solution(1015585720763781488)
XLA Ops:
  0.0 0.0 copy-start.2
  0.0 0.0 copy-start.1
  0.0 0.0 copy-start
  0.0 4.1 %reshape.6.x = bf16[128,8192]{1,0:T(8,128)(2,1)} reshape(bf16[64,2,8192]{2,1,0:T(2,128)(2,1)} %param.4) | data formatting | bytes 4194304 | tf_op jit(solution)/shard_map/reshape | solution.py:435
  4.1 0.0 copy-done.2
  4.1 0.0 copy-done.1
  4.2 0.0 copy-done
  4.2 99.7 %shard_map.46 = bf16[128,8192]{1,0:T(8,128)(2,1)S(1)} custom-call(bf16[128,8192]{1,0:T(8,128)(2,1)} %reshape.6.x, s32[4,128]{1,0:T(4,128)S(1)} %copy-done, f32[4,128]{1,0:T(4,128)S(1)} %copy-done.1, f32[4,128]{1,0:T(4,128)S(1)} %copy-done.2), custom_call_target="tpu_custom_call" | custom-call | tf_op jit(solution)/shard_map/pallas_call | solution.py:426
  103.9 2.6 %reshape.7 = bf16[64,2,8192]{2,1,0:T(2,128)(2,1)} reshape(bf16[128,8192]{1,0:T(8,128)(2,1)S(1)} %shard_map.46) | data formatting | bytes 4194304 | tf_op jit(solution)/shard_map/reshape | solution.py:436
Async XLA Ops:
  0.0 4.1 %copy-start.2 = (f32[4,128]{1,0:T(4,128)S(1)}, f32[4,128]{1,0:T(4,128)}, u32[]{:S(2)}) copy-start(f32[4,128]{1,0:T(4,128)} %spread.1) | copy-start | bytes 6148
  0.0 4.1 %copy-start.1 = (f32[4,128]{1,0:T(4,128)S(1)}, f32[4,128]{1,0:T(4,128)}, u32[]{:S(2)}) copy-start(f32[4,128]{1,0:T(4,128)} %datum.1) | copy-start | bytes 6148
  0.0 4.1 %copy-start = (s32[4,128]{1,0:T(4,128)S(1)}, s32[4,128]{1,0:T(4,128)}, u32[]{:S(2)}) copy-start(s32[4,128]{1,0:T(4,128)} %loc.1) | copy-start | bytes 6148

commit v2 on v1

--- a/solution.py
+++ b/solution.py
@@ -51,9 +51,9 @@
 
 def kernel(
     dims, x, loc, datum, spread, y,
-    held, anom, means, hot, scaled, gram, r1, s1, r2, s2, r3, full,
+    near, places, picked, raw, held, anom, means, hot, scaled, gram, r1, s1, r2, s2, r3, full,
     sys_f, u_f, z_f, his, los, wts, base, outs,
-    a_send, a_recv, own_sem, c_send, c_recv, q_send, q_recv, z_send, z_recv,
+    near_sem, l_send, l_recv, p_send, p_recv, a_send, a_recv, own_sem, c_send, c_recv, q_send, q_recv, z_send, z_recv,
     zg_send, zg_recv, qg_send, qg_recv, cg_send, cg_recv, o_send, o_recv,
 ):
     n, nz, members, fields, cells, mloc, grid_cells = dims
@@ -67,6 +67,9 @@
     core, chip = lax.rem(me, 2), lax.div(me, 2)
     mate = me + 1 - 2 * core
 
+    fetch = pltpu.make_async_copy(x, near, near_sem)
+    fetch.start()
+
     barrier = pltpu.get_barrier_semaphore()
     for d in range(1, n):
         pl.semaphore_signal(barrier, inc=1, device_id={"mem": lax.rem(me + d, n)}, device_id_type=MESH)
@@ -83,75 +86,85 @@
     def share(p):
         return pl.ds(pl.multiple_of(p * mloc, mloc), mloc)
 
-    def send_in(d, _):
-        p = lax.rem(me + d, n)
-        remote(x.at[:, col(p)], held.at[block(me)], a_send.at[d], a_recv.at[d], {"mem": p}).start()
-        return 0
-
-    lax.fori_loop(1, n, send_in, 0)
-    own = pltpu.make_async_copy(x.at[:, col(me)], held.at[block(me)], own_sem)
-    own.start()
-
-    first_cell = (mz * n + me) * cells
+    def peer(j):
+        return lax.rem(chip + lax.div(j, 2), nq) * 2 + lax.rem(core + j, 2)
+
+    def source(j):
+        return lax.rem(chip + nq - lax.div(j, 2), nq) * 2 + lax.rem(core + j, 2)
+
+    def place_copy(p, at):
+        return remote(loc, places.at[at], l_send.at[p], l_recv.at[at], {"mem": p})
+
+    def send_places(j, _):
+        place_copy(peer(j), me).start()
+        return 0
+
+    lax.fori_loop(1, n, send_places, 0)
+    places[me] = loc[...]
     obs_rows = loc.shape[0]
     obs = obs_rows * LANES
-    v = loc[...]
-    slots = v - first_cell
-    for f in range(1, fields):
-        slots = slots + jnp.where(v >= f * grid_cells, cells - grid_cells, 0)
-
-    def build(i, _):
-        at = pl.ds(pl.multiple_of(i * LANES, LANES), LANES)
-        cell = iota((LANES, LANES), 0) + i * LANES
-        for r in range(obs_rows):
-            hot[at, r * LANES:(r + 1) * LANES] = jnp.where(cell == slots[r:r + 1, :], 1.0, 0.0).astype(BF)
-        return 0
-
-    lax.fori_loop(0, fields * cells // LANES, build, 0)
-
-    means[...] = jnp.zeros_like(means)
-
-    def take(p):
-        got = held[block(p), :]
-        for f in range(fields):
-            pick = jnp.where(iota((mloc, rows), 1) == iota((mloc, rows), 0) * fields + f, 1.0, 0.0).astype(BF)
-            lines = nn(pick, got)
-            at = slice(f * cells, (f + 1) * cells)
-            anom[share(p), at] = lines.astype(BF)
-            means[:, at] += jnp.sum(lines, axis=0, keepdims=True)
-
-    own.wait()
-    take(me)
-
-    def arrive(d, _):
-        p = lax.rem(me + n - d, n)
-        remote(x.at[:, col(p)], held.at[block(p)], a_send.at[d], a_recv.at[d], {"mem": p}).wait_recv()
-        take(p)
-        return 0
-
-    lax.fori_loop(1, n, arrive, 0)
-    means[...] = means[...] / members
-
-    def centre(i, _):
-        at = pl.ds(pl.multiple_of(i * 64, 64), 64)
-        lines = (anom[at, :].astype(F32) - means[...]).astype(BF)
-        anom[at, :] = lines
-        return 0
-
-    lax.fori_loop(0, members // 64, centre, 0)
+    fetch.wait()
+
+    def choose(p):
+        v = places[p]
+        field = jnp.zeros_like(v)
+        for f in range(1, fields):
+            field = field + jnp.where(v >= f * grid_cells, 1, 0)
+        slots = v - field * grid_cells - (mz * n + p) * cells
+
+        def build(i, _):
+            at = pl.ds(pl.multiple_of(i * LANES, LANES), LANES)
+            cell = iota((LANES, LANES), 0) + i * LANES
+            for r in range(obs_rows):
+                hot[at, r * LANES:(r + 1) * LANES] = jnp.where(cell == slots[r:r + 1, :], 1.0, 0.0).astype(BF)
+            return 0
+
+        lax.fori_loop(0, cells // LANES, build, 0)
+        both = nn(near[:, col(p)], hot[...])
+        wanted = jnp.concatenate([field[r:r + 1, :] for r in range(obs_rows)], axis=1)
+        both = jnp.where((iota((rows, obs), 0) & (fields - 1)) == wanted, both, 0.0).astype(BF)
+        low = iota((mloc, rows), 0) * fields
+        join = jnp.where((iota((mloc, rows), 1) >= low) & (iota((mloc, rows), 1) < low + fields), 1.0, 0.0)
+        return nn(join.astype(BF), both).astype(BF)
+
+    def pick_copy(p, at):
+        return remote(picked.at[p], raw.at[share(at)], p_send.at[p], p_recv.at[at], {"mem": p})
+
+    def send_picked(j, _):
+        p = peer(j)
+        place_copy(p, p).wait_recv()
+        picked[p] = choose(p)
+        pick_copy(p, me).start()
+        return 0
+
+    lax.fori_loop(1, n, send_picked, 0)
+    raw[share(me), :] = choose(me)
+
+    def get_picked(j, _):
+        p = source(j)
+        pick_copy(p, p).wait_recv()
+        return 0
+
+    lax.fori_loop(1, n, get_picked, 0)
 
     errors = jnp.concatenate([spread[r:r + 1, :] for r in range(obs_rows)], axis=1)
     values = jnp.concatenate([datum[r:r + 1, :] for r in range(obs_rows)], axis=1)
     inverse = 1.0 / (errors * norm_factor)
-    mean_obs = row_times(means[...], hot[...])
+
+    def add_rows(i, carry):
+        at = pl.ds(pl.multiple_of(i * 64, 64), 64)
+        return carry + jnp.sum(raw[at, :].astype(F32), axis=0, keepdims=True)
+
+    mean_obs = lax.fori_loop(0, members // 64, add_rows, jnp.zeros((1, obs), F32)) / members
     innovation = ((values - mean_obs) / errors).astype(BF)
 
-    def pick_rows(i, _):
-        at = pl.ds(pl.multiple_of(i * 256, 256), 256)
-        scaled[at, :] = (nn(anom[at, :], hot[...]) * inverse).astype(BF)
-        return 0
-
-    lax.fori_loop(0, members // 256, pick_rows, 0)
+    def scale_rows(i, _):
+        at = pl.ds(pl.multiple_of(i * 64, 64), 64)
+        anomaly = (raw[at, :].astype(F32) - mean_obs).astype(BF)
+        scaled[at, :] = (anomaly.astype(F32) * inverse).astype(BF)
+        return 0
+
+    lax.fori_loop(0, members // 64, scale_rows, 0)
     spread16 = jnp.where(iota((16, obs), 0) == 0, innovation.astype(F32), 0.0).astype(BF)
     projected = jnp.sum(nt(spread16, scaled[...]), axis=0, keepdims=True)
 
@@ -196,12 +209,40 @@
         acc = acc + r2[d]
     s2[...] = acc
 
+    def block_copy(p, at):
+        return remote(x.at[:, col(p)], held.at[block(at)], a_send.at[p], a_recv.at[at], {"mem": p})
+
+    def take(p):
+        got = held[block(p), :]
+        for f in range(fields):
+            pick = jnp.where(iota((mloc, rows), 1) == iota((mloc, rows), 0) * fields + f, 1.0, 0.0).astype(BF)
+            lines = nn(pick, got)
+            at = slice(f * cells, (f + 1) * cells)
+            anom[share(p), at] = lines.astype(BF)
+            means[:, at] += jnp.sum(lines, axis=0, keepdims=True)
+
+    def send_block(j, _):
+        block_copy(peer(j), me).start()
+        return 0
+
+    def get_block(j, _):
+        p = source(j)
+        block_copy(p, p).wait_recv()
+        take(p)
+        return 0
+
     def line_of(d):
         k = lax.rem(mz + d, nz)
         return remote(s2.at[cut(k * piece, piece)], r3.at[d], z_send.at[d], z_recv.at[d], {"cell": k})
 
     for d in range(1, nz):
         line_of(d).start()
+    lax.fori_loop(1, n, send_block, 0)
+    own = pltpu.make_async_copy(x.at[:, col(me)], held.at[block(me)], own_sem)
+    own.start()
+    means[...] = jnp.zeros_like(means)
+    own.wait()
+    take(me)
     acc = s2[cut(mz * piece, piece), :]
     for d in range(1, nz):
         line_of(d).wait_recv()
@@ -215,6 +256,7 @@
 
     for d in range(1, nz):
         line_back(d, mz).start()
+    get_block(1, 0)
     for d in range(1, nz):
         line_back(d, lax.rem(mz + nz - d, nz)).wait_recv()
 
@@ -330,6 +372,16 @@
 
     times(IQ, IZ + NS_ITERS // 2 - 2, final)
 
+    lax.fori_loop(2, n, get_block, 0)
+    means[...] = means[...] / members
+
+    def centre(i, _):
+        at = pl.ds(pl.multiple_of(i * 64, 64), 64)
+        anom[at, :] = (anom[at, :].astype(F32) - means[...]).astype(BF)
+        return 0
+
+    lax.fori_loop(0, members // 64, centre, 0)
+
     root = 1.0 / jnp.sqrt(norm_scale)
 
     def weigh(i, carry):
@@ -356,13 +408,13 @@
             out = part if out is None else jnp.where(field == f, part, out)
         return out.astype(BF)
 
-    def out_copy(d, p, to):
-        return remote(outs.at[p], y.at[:, col(to)], o_send.at[d], o_recv.at[d], {"mem": p})
-
-    def send_out(d, _):
-        p = lax.rem(me + d, n)
+    def out_copy(p, at):
+        return remote(outs.at[p], y.at[:, col(at)], o_send.at[p], o_recv.at[at], {"mem": p})
+
+    def send_out(j, _):
+        p = peer(j)
         outs[p] = make(p)
-        out_copy(d, p, me).start()
+        out_copy(p, me).start()
         return 0
 
     lax.fori_loop(1, n, send_out, 0)
@@ -370,18 +422,20 @@
     own = pltpu.make_async_copy(outs.at[me], y.at[:, col(me)], own_sem)
     own.start()
 
-    def finish_out(d, _):
-        p = lax.rem(me + n - d, n)
-        out_copy(d, p, p).wait_recv()
+    def finish_out(j, _):
+        p = source(j)
+        out_copy(p, p).wait_recv()
         return 0
 
     lax.fori_loop(1, n, finish_out, 0)
     own.wait()
 
-    def sent(d, _):
-        p = lax.rem(me + d, n)
-        remote(x.at[:, col(p)], held.at[block(me)], a_send.at[d], a_recv.at[d], {"mem": p}).wait_send()
-        out_copy(d, p, me).wait_send()
+    def sent(j, _):
+        p = peer(j)
+        place_copy(p, me).wait_send()
+        pick_copy(p, me).wait_send()
+        block_copy(p, me).wait_send()
+        out_copy(p, me).wait_send()
         return 0
 
     lax.fori_loop(1, n, sent, 0)
@@ -412,14 +466,17 @@
     vm, dma = pltpu.VMEM, pltpu.SemaphoreType.DMA
     square = (members, members)
     scratch = [
+        vm((rows, width), BF), vm((n,) + measurement_location.shape, jnp.int32),
+        vm((n, mloc, obs), BF), vm((members, obs), BF),
         vm((n * rows, cells), BF), vm((members, fields * cells), BF), vm((1, fields * cells), F32),
-        vm((fields * cells, obs), BF), vm((members, obs), BF),
+        vm((cells, obs), BF), vm((members, obs), BF),
         vm((total, LANES), F32), vm((half, LANES), F32), vm((half, LANES), F32),
         vm((nq, quart, LANES), F32), vm((quart, LANES), F32), vm((nz, piece, LANES), F32),
         vm((total, LANES), F32),
         vm(square, F32), vm(square, F32), vm(square, F32),
         vm((zslots,) + square, BF), vm((zslots,) + square, BF), vm(square, BF),
         vm((1, fields * cells), F32), vm((n, rows, cells), BF),
+        dma, dma((n,)), dma((n,)), dma((n,)), dma((n,)),
         dma((n,)), dma((n,)), dma, dma, dma, dma((nq,)), dma((nq,)), dma((nz,)), dma((nz,)),
         dma((nz,)), dma((nz,)), dma((nq,)), dma((nq,)), dma((nq,)), dma((nq,)), dma((n,)), dma((n,)),
     ]

time: 108 us -> 112 us (1.037); the launches traced: 107 us -> 112 us
  Pallas kernels: 99.7 us -> 105 us
    pallas_call x1, Pallas kernels: 99.7 us -> 105 us  [local(): pl.pallas_call(functools.partial(kernel, dims), out_shape=jax.ShapeDtypeS...]
where the time goes in v2:
time: 112 us
  Pallas kernels  105 us (94%)
  local copies, waits for them, and re-layouts  6.78 us (6%)
    pallas_call x1, Pallas kernels, local(): pl.pallas_call(functools.partial(kernel, dims), out_shape=jax.ShapeDtypeS...  105 us
    reshape x1, local copies, waits for them, and re-layouts, local(): prior_ensemble.reshape(rows, width)  4.14 us
    reshape x1, local copies, waits for them, and re-layouts, local(): return out.reshape(mloc, fields, width)  2.63 us

profile of v2, /device:TPU:0, one launch (start us, length us, event | category | flops | bytes accessed | tf_op | source)
XLA Modules:
  0.0 111.9 jit_solution(8575154169720327467)
XLA Ops:
  0.0 0.0 copy-start.2
  0.0 0.0 copy-start.1
  0.0 0.0 copy-start
  0.0 4.1 %reshape.6.x = bf16[128,8192]{1,0:T(8,128)(2,1)} reshape(bf16[64,2,8192]{2,1,0:T(2,128)(2,1)} %param.4) | data formatting | bytes 4194304 | tf_op jit(solution)/shard_map/reshape | solution.py:492
  4.1 0.0 copy-done.2
  4.1 0.0 copy-done.1
  4.2 0.0 copy-done
  4.2 105.1 %shard_map.46 = bf16[128,8192]{1,0:T(8,128)(2,1)S(1)} custom-call(bf16[128,8192]{1,0:T(8,128)(2,1)} %reshape.6.x, s32[4,128]{1,0:T(4,128)S(1)} %copy-done, f32[4,128]{1,0:T(4,128)S(1)} %copy-done.1, f32[4,128]{1,0:T(4,128)S(1)} %copy-done.2), custom_call_target="tpu_custom_call" | custom-call | tf_op jit(solution)/shard_map/pallas_call | solution.py:483
  109.3 2.6 %reshape.7 = bf16[64,2,8192]{2,1,0:T(2,128)(2,1)} reshape(bf16[128,8192]{1,0:T(8,128)(2,1)S(1)} %shard_map.46) | data formatting | bytes 4194304 | tf_op jit(solution)/shard_map/reshape | solution.py:493
Async XLA Ops:
  0.0 4.1 %copy-start.2 = (f32[4,128]{1,0:T(4,128)S(1)}, f32[4,128]{1,0:T(4,128)}, u32[]{:S(2)}) copy-start(f32[4,128]{1,0:T(4,128)} %spread.1) | copy-start | bytes 6148
  0.0 4.1 %copy-start.1 = (f32[4,128]{1,0:T(4,128)S(1)}, f32[4,128]{1,0:T(4,128)}, u32[]{:S(2)}) copy-start(f32[4,128]{1,0:T(4,128)} %datum.1) | copy-start | bytes 6148
  0.0 4.1 %copy-start = (s32[4,128]{1,0:T(4,128)S(1)}, s32[4,128]{1,0:T(4,128)}, u32[]{:S(2)}) copy-start(s32[4,128]{1,0:T(4,128)} %loc.1) | copy-start | bytes 6148

commit v3 on v2

--- a/solution.py
+++ b/solution.py
@@ -237,7 +237,7 @@
 
     for d in range(1, nz):
         line_of(d).start()
-    lax.fori_loop(1, n, send_block, 0)
+    send_block(1, 0)
     own = pltpu.make_async_copy(x.at[:, col(me)], held.at[block(me)], own_sem)
     own.start()
     means[...] = jnp.zeros_like(means)
@@ -275,6 +275,7 @@
         q = lax.rem(chip + nq - d, nq)
         plane_back(d, q).wait_recv()
         pair_back(d, core, q).start()
+    lax.fori_loop(2, n, send_block, 0)
     for d in range(nq):
         pair_back(d, 1 - core, lax.rem(chip + nq - d, nq)).wait_recv()
 

time: 112 us -> 103 us (0.920)
  Pallas kernels: 105 us -> 95.7 us
    pallas_call x1, Pallas kernels: 105 us -> 95.7 us  [local(): pl.pallas_call(functools.partial(kernel, dims), out_shape=jax.ShapeDtypeS...]
where the time goes in v3:
time: 103 us
  Pallas kernels  95.7 us (93%)
  local copies, waits for them, and re-layouts  6.78 us (7%)
    pallas_call x1, Pallas kernels, local(): pl.pallas_call(functools.partial(kernel, dims), out_shape=jax.ShapeDtypeS...  95.7 us
    reshape x1, local copies, waits for them, and re-layouts, local(): prior_ensemble.reshape(rows, width)  4.14 us
    reshape x1, local copies, waits for them, and re-layouts, local(): return out.reshape(mloc, fields, width)  2.63 us

profile of v3, /device:TPU:0, one launch (start us, length us, event | category | flops | bytes accessed | tf_op | source)
XLA Modules:
  0.0 102.5 jit_solution(10543586563043572918)
XLA Ops:
  0.0 0.0 copy-start.2
  0.0 0.0 copy-start.1
  0.0 0.0 copy-start
  0.0 4.1 %reshape.6.x = bf16[128,8192]{1,0:T(8,128)(2,1)} reshape(bf16[64,2,8192]{2,1,0:T(2,128)(2,1)} %param.4) | data formatting | bytes 4194304 | tf_op jit(solution)/shard_map/reshape | solution.py:493
  4.1 0.0 copy-done.2
  4.1 0.0 copy-done.1
  4.2 0.0 copy-done
  4.2 95.7 %shard_map.46 = bf16[128,8192]{1,0:T(8,128)(2,1)S(1)} custom-call(bf16[128,8192]{1,0:T(8,128)(2,1)} %reshape.6.x, s32[4,128]{1,0:T(4,128)S(1)} %copy-done, f32[4,128]{1,0:T(4,128)S(1)} %copy-done.1, f32[4,128]{1,0:T(4,128)S(1)} %copy-done.2), custom_call_target="tpu_custom_call" | custom-call | tf_op jit(solution)/shard_map/pallas_call | solution.py:484
  99.9 2.6 %reshape.7 = bf16[64,2,8192]{2,1,0:T(2,128)(2,1)} reshape(bf16[128,8192]{1,0:T(8,128)(2,1)S(1)} %shard_map.46) | data formatting | bytes 4194304 | tf_op jit(solution)/shard_map/reshape | solution.py:494
Async XLA Ops:
  0.0 4.1 %copy-start.2 = (f32[4,128]{1,0:T(4,128)S(1)}, f32[4,128]{1,0:T(4,128)}, u32[]{:S(2)}) copy-start(f32[4,128]{1,0:T(4,128)} %spread.1) | copy-start | bytes 6148
  0.0 4.1 %copy-start.1 = (f32[4,128]{1,0:T(4,128)S(1)}, f32[4,128]{1,0:T(4,128)}, u32[]{:S(2)}) copy-start(f32[4,128]{1,0:T(4,128)} %datum.1) | copy-start | bytes 6148
  0.0 4.1 %copy-start = (s32[4,128]{1,0:T(4,128)S(1)}, s32[4,128]{1,0:T(4,128)}, u32[]{:S(2)}) copy-start(s32[4,128]{1,0:T(4,128)} %loc.1) | copy-start | bytes 6148

commit v4 on v3

--- a/solution.py
+++ b/solution.py
@@ -312,13 +312,11 @@
         los[slot, at, :] = (val - hi.astype(F32)).astype(BF)
 
     def times(a, b, finish):
-        def go(i, _):
-            at = pl.ds(pl.multiple_of(i * step, step), step)
+        right = jnp.concatenate([his[b], los[b], his[b]], axis=0)
+        for i in range(chunks):
+            at = slice(i * step, (i + 1) * step)
             ah, al = his[a, at, :], los[a, at, :]
-            finish(at, i, nn(ah, his[b]) + nn(ah, los[b]) + nn(al, his[b]))
-            return 0
-
-        lax.fori_loop(0, chunks, go, 0)
+            finish(at, i, nn(jnp.concatenate([ah, ah, al], axis=1), right))
 
     def scale(i, _):
         at = pl.ds(pl.multiple_of(i * 64, 64), 64)

time: 103 us -> 98.8 us (0.959)
  Pallas kernels: 95.7 us -> 91.5 us
    pallas_call x1, Pallas kernels: 95.7 us -> 91.5 us  [local(): pl.pallas_call(functools.partial(kernel, dims), out_shape=jax.ShapeDtypeS...]
where the time goes in v4:
time: 98.8 us; the launch traced here: 98.2 us
  Pallas kernels  91.5 us (93%)
  local copies, waits for them, and re-layouts  6.78 us (7%)
    pallas_call x1, Pallas kernels, local(): pl.pallas_call(functools.partial(kernel, dims), out_shape=jax.ShapeDtypeS...  91.5 us
    reshape x1, local copies, waits for them, and re-layouts, local(): prior_ensemble.reshape(rows, width)  4.14 us
    reshape x1, local copies, waits for them, and re-layouts, local(): return out.reshape(mloc, fields, width)  2.63 us

profile of v4, /device:TPU:0, one launch (start us, length us, event | category | flops | bytes accessed | tf_op | source)
XLA Modules:
  0.0 98.2 jit_solution(6663243959206524133)
XLA Ops:
  0.0 0.0 copy-start.2
  0.0 0.0 copy-start.1
  0.0 0.0 copy-start
  0.0 4.1 %reshape.6.x = bf16[128,8192]{1,0:T(8,128)(2,1)} reshape(bf16[64,2,8192]{2,1,0:T(2,128)(2,1)} %param.4) | data formatting | bytes 4194304 | tf_op jit(solution)/shard_map/reshape | solution.py:491
  4.1 0.0 copy-done.2
  4.1 0.0 copy-done.1
  4.2 0.0 copy-done
  4.2 91.5 %shard_map.46 = bf16[128,8192]{1,0:T(8,128)(2,1)S(1)} custom-call(bf16[128,8192]{1,0:T(8,128)(2,1)} %reshape.6.x, s32[4,128]{1,0:T(4,128)S(1)} %copy-done, f32[4,128]{1,0:T(4,128)S(1)} %copy-done.1, f32[4,128]{1,0:T(4,128)S(1)} %copy-done.2), custom_call_target="tpu_custom_call" | custom-call | tf_op jit(solution)/shard_map/pallas_call | solution.py:482
  95.6 2.6 %reshape.7 = bf16[64,2,8192]{2,1,0:T(2,128)(2,1)} reshape(bf16[128,8192]{1,0:T(8,128)(2,1)S(1)} %shard_map.46) | data formatting | bytes 4194304 | tf_op jit(solution)/shard_map/reshape | solution.py:492
Async XLA Ops:
  0.0 4.1 %copy-start.2 = (f32[4,128]{1,0:T(4,128)S(1)}, f32[4,128]{1,0:T(4,128)}, u32[]{:S(2)}) copy-start(f32[4,128]{1,0:T(4,128)} %spread.1) | copy-start | bytes 6148
  0.0 4.1 %copy-start.1 = (f32[4,128]{1,0:T(4,128)S(1)}, f32[4,128]{1,0:T(4,128)}, u32[]{:S(2)}) copy-start(f32[4,128]{1,0:T(4,128)} %datum.1) | copy-start | bytes 6148
  0.0 4.1 %copy-start = (s32[4,128]{1,0:T(4,128)S(1)}, s32[4,128]{1,0:T(4,128)}, u32[]{:S(2)}) copy-start(s32[4,128]{1,0:T(4,128)} %loc.1) | copy-start | bytes 6148

commit v5 on v4

--- a/solution.py
+++ b/solution.py
@@ -40,19 +40,10 @@
     return hi, mid, lo
 
 
-def row_times(v, mat):
-    parts = thirds(v)
-    row = iota((16, v.shape[1]), 0)
-    stack = jnp.zeros((16, v.shape[1]), F32)
-    for i, part in enumerate(parts):
-        stack = jnp.where(row == i, part.astype(F32), stack)
-    return jnp.sum(nn(stack.astype(BF), mat), axis=0, keepdims=True)
-
-
 def kernel(
     dims, x, loc, datum, spread, y,
-    near, places, picked, raw, held, anom, means, hot, scaled, gram, r1, s1, r2, s2, r3, full,
-    sys_f, u_f, z_f, his, los, wts, base, outs,
+    near, places, picked, raw, held, anom, means, scaled, gram, r1, s1, r2, s2, r3, full,
+    sys_f, u_f, z_f, his, los, wts, mix, outs,
     near_sem, l_send, l_recv, p_send, p_recv, a_send, a_recv, own_sem, c_send, c_recv, q_send, q_recv, z_send, z_recv,
     zg_send, zg_recv, qg_send, qg_recv, cg_send, cg_recv, o_send, o_recv,
 ):
@@ -112,15 +103,9 @@
             field = field + jnp.where(v >= f * grid_cells, 1, 0)
         slots = v - field * grid_cells - (mz * n + p) * cells
 
-        def build(i, _):
-            at = pl.ds(pl.multiple_of(i * LANES, LANES), LANES)
-            cell = iota((LANES, LANES), 0) + i * LANES
-            for r in range(obs_rows):
-                hot[at, r * LANES:(r + 1) * LANES] = jnp.where(cell == slots[r:r + 1, :], 1.0, 0.0).astype(BF)
-            return 0
-
-        lax.fori_loop(0, cells // LANES, build, 0)
-        both = nn(near[:, col(p)], hot[...])
+        slot = jnp.concatenate([slots[r:r + 1, :] for r in range(obs_rows)], axis=1)
+        hot = jnp.where(iota((cells, obs), 0) == slot, 1.0, 0.0).astype(BF)
+        both = nn(near[:, col(p)], hot)
         wanted = jnp.concatenate([field[r:r + 1, :] for r in range(obs_rows)], axis=1)
         both = jnp.where((iota((rows, obs), 0) & (fields - 1)) == wanted, both, 0.0).astype(BF)
         low = iota((mloc, rows), 0) * fields
@@ -130,15 +115,24 @@
     def pick_copy(p, at):
         return remote(picked.at[p], raw.at[share(at)], p_send.at[p], p_recv.at[at], {"mem": p})
 
-    def send_picked(j, _):
-        p = peer(j)
+    def send_picked(i, _):
+        p, q = peer(2 * i + 1), peer(2 * i + 2)
         place_copy(p, p).wait_recv()
-        picked[p] = choose(p)
+        place_copy(q, q).wait_recv()
+        first, second = choose(p), choose(q)
+        picked[p] = first
+        picked[q] = second
         pick_copy(p, me).start()
-        return 0
-
-    lax.fori_loop(1, n, send_picked, 0)
-    raw[share(me), :] = choose(me)
+        pick_copy(q, me).start()
+        return 0
+
+    lax.fori_loop(0, n // 2 - 1, send_picked, 0)
+    p = peer(n - 1)
+    place_copy(p, p).wait_recv()
+    first, second = choose(p), choose(me)
+    picked[p] = first
+    pick_copy(p, me).start()
+    raw[share(me), :] = second
 
     def get_picked(j, _):
         p = source(j)
@@ -371,7 +365,15 @@
 
     times(IQ, IZ + NS_ITERS // 2 - 2, final)
 
-    lax.fori_loop(2, n, get_block, 0)
+    def get_two(i, _):
+        p, q = source(2 * i), source(2 * i + 1)
+        block_copy(p, p).wait_recv()
+        block_copy(q, q).wait_recv()
+        take(p)
+        take(q)
+        return 0
+
+    lax.fori_loop(1, n // 2, get_two, 0)
     means[...] = means[...] / members
 
     def centre(i, _):
@@ -392,18 +394,24 @@
         return carry + jnp.sum(shift * w.astype(F32), axis=0, keepdims=True)
 
     mixed = lax.fori_loop(0, members // 64, weigh, jnp.zeros((1, members), F32))
-    base[...] = means[...] + row_times(mixed, anom[...])
+    line = iota((16, members), 0)
+    stack = jnp.zeros((16, members), F32)
+    for i, part in enumerate(thirds(mixed)):
+        stack = jnp.where(line == i, part.astype(F32), stack)
+    mix[...] = stack.astype(BF)
 
     def make(p):
         double = jnp.where(
             (iota((rows, mloc), 0) >= iota((rows, mloc), 1) * fields)
             & (iota((rows, mloc), 0) < iota((rows, mloc), 1) * fields + fields), 1.0, 0.0).astype(BF)
-        w2 = nn(double, wts[share(p), :]).astype(BF)
+        w2 = jnp.concatenate([nn(double, wts[share(p), :]).astype(BF), mix[...]], axis=0)
         field = iota((rows, cells), 0) & (fields - 1)
         out = None
         for f in range(fields):
             at = slice(f * cells, (f + 1) * cells)
-            part = nn(w2, anom[:, at]) + base[:, at]
+            part = nn(w2, anom[:, at])
+            shift = jnp.sum(part[rows:, :], axis=0, keepdims=True)
+            part = part[:rows, :] + (means[:, at] + shift)
             out = part if out is None else jnp.where(field == f, part, out)
         return out.astype(BF)
 
@@ -468,13 +476,13 @@
         vm((rows, width), BF), vm((n,) + measurement_location.shape, jnp.int32),
         vm((n, mloc, obs), BF), vm((members, obs), BF),
         vm((n * rows, cells), BF), vm((members, fields * cells), BF), vm((1, fields * cells), F32),
-        vm((cells, obs), BF), vm((members, obs), BF),
+        vm((members, obs), BF),
         vm((total, LANES), F32), vm((half, LANES), F32), vm((half, LANES), F32),
         vm((nq, quart, LANES), F32), vm((quart, LANES), F32), vm((nz, piece, LANES), F32),
         vm((total, LANES), F32),
         vm(square, F32), vm(square, F32), vm(square, F32),
         vm((zslots,) + square, BF), vm((zslots,) + square, BF), vm(square, BF),
-        vm((1, fields * cells), F32), vm((n, rows, cells), BF),
+        vm((16, members), BF), vm((n, rows, cells), BF),
         dma, dma((n,)), dma((n,)), dma((n,)), dma((n,)),
         dma((n,)), dma((n,)), dma, dma, dma, dma((nq,)), dma((nq,)), dma((nz,)), dma((nz,)),
         dma((nz,)), dma((nz,)), dma((nq,)), dma((nq,)), dma((nq,)), dma((nq,)), dma((n,)), dma((n,)),

time: 98.8 us -> 97 us (0.982)
  Pallas kernels: 91.5 us -> 89.7 us
    pallas_call x1, Pallas kernels: 91.5 us -> 89.7 us  [local(): pl.pallas_call(functools.partial(kernel, dims), out_shape=jax.ShapeDtypeS...]
where the time goes in v5:
time: 97 us; the launch traced here: 96.5 us
  Pallas kernels  89.7 us (92%)
  local copies, waits for them, and re-layouts  6.78 us (7%)
    pallas_call x1, Pallas kernels, local(): pl.pallas_call(functools.partial(kernel, dims), out_shape=jax.ShapeDtypeS...  89.7 us
    reshape x1, local copies, waits for them, and re-layouts, local(): prior_ensemble.reshape(rows, width)  4.14 us
    reshape x1, local copies, waits for them, and re-layouts, local(): return out.reshape(mloc, fields, width)  2.63 us

profile of v5, /device:TPU:0, one launch (start us, length us, event | category | flops | bytes accessed | tf_op | source)
XLA Modules:
  0.0 96.5 jit_solution(12702619918606973181)
XLA Ops:
  0.0 0.0 copy-start.2
  0.0 0.0 copy-start.1
  0.0 0.0 copy-start
  0.0 4.1 %reshape.6.x = bf16[128,8192]{1,0:T(8,128)(2,1)} reshape(bf16[64,2,8192]{2,1,0:T(2,128)(2,1)} %param.4) | data formatting | bytes 4194304 | tf_op jit(solution)/shard_map/reshape | solution.py:499
  4.1 0.0 copy-done.2
  4.1 0.0 copy-done.1
  4.2 0.0 copy-done
  4.2 89.7 %shard_map.46 = bf16[128,8192]{1,0:T(8,128)(2,1)S(1)} custom-call(bf16[128,8192]{1,0:T(8,128)(2,1)} %reshape.6.x, s32[4,128]{1,0:T(4,128)S(1)} %copy-done, f32[4,128]{1,0:T(4,128)S(1)} %copy-done.1, f32[4,128]{1,0:T(4,128)S(1)} %copy-done.2), custom_call_target="tpu_custom_call" | custom-call | tf_op jit(solution)/shard_map/pallas_call | solution.py:490
  93.9 2.6 %reshape.7 = bf16[64,2,8192]{2,1,0:T(2,128)(2,1)} reshape(bf16[128,8192]{1,0:T(8,128)(2,1)S(1)} %shard_map.46) | data formatting | bytes 4194304 | tf_op jit(solution)/shard_map/reshape | solution.py:500
Async XLA Ops:
  0.0 4.1 %copy-start.2 = (f32[4,128]{1,0:T(4,128)S(1)}, f32[4,128]{1,0:T(4,128)}, u32[]{:S(2)}) copy-start(f32[4,128]{1,0:T(4,128)} %spread.1) | copy-start | bytes 6148
  0.0 4.1 %copy-start.1 = (f32[4,128]{1,0:T(4,128)S(1)}, f32[4,128]{1,0:T(4,128)}, u32[]{:S(2)}) copy-start(f32[4,128]{1,0:T(4,128)} %datum.1) | copy-start | bytes 6148
  0.0 4.1 %copy-start = (s32[4,128]{1,0:T(4,128)S(1)}, s32[4,128]{1,0:T(4,128)}, u32[]{:S(2)}) copy-start(s32[4,128]{1,0:T(4,128)} %loc.1) | copy-start | bytes 6148

commit v6 on v5

--- a/solution.py
+++ b/solution.py
@@ -134,6 +134,34 @@
     pick_copy(p, me).start()
     raw[share(me), :] = second
 
+    def block_copy(p, at):
+        return remote(x.at[:, col(p)], held.at[block(at)], a_send.at[p], a_recv.at[at], {"mem": p})
+
+    def take(p):
+        got = held[block(p), :]
+        for f in range(fields):
+            pick = jnp.where(iota((mloc, rows), 1) == iota((mloc, rows), 0) * fields + f, 1.0, 0.0).astype(BF)
+            lines = nn(pick, got)
+            at = slice(f * cells, (f + 1) * cells)
+            anom[share(p), at] = lines.astype(BF)
+            means[:, at] += jnp.sum(lines, axis=0, keepdims=True)
+
+    def send_block(j, _):
+        block_copy(peer(j), me).start()
+        return 0
+
+    def get_block(j, _):
+        p = source(j)
+        block_copy(p, p).wait_recv()
+        take(p)
+        return 0
+
+    send_block(1, 0)
+    send_block(2, 0)
+    own = pltpu.make_async_copy(x.at[:, col(me)], held.at[block(me)], own_sem)
+    own.start()
+    means[...] = jnp.zeros_like(means)
+
     def get_picked(j, _):
         p = source(j)
         pick_copy(p, p).wait_recv()
@@ -185,6 +213,8 @@
 
     go = remote(gram.at[cut((1 - core) * half, half)], r1, c_send, c_recv, {"mem": mate})
     go.start()
+    own.wait()
+    take(me)
     go.wait_recv()
     s1[...] = gram[cut(core * half, half), :] + r1[...]
 
@@ -197,46 +227,21 @@
 
     for d in range(1, nq):
         plane(d).start()
+    get_block(1, 0)
     acc = s1[cut(chip * quart, quart), :]
     for d in range(1, nq):
         plane(d).wait_recv()
         acc = acc + r2[d]
     s2[...] = acc
 
-    def block_copy(p, at):
-        return remote(x.at[:, col(p)], held.at[block(at)], a_send.at[p], a_recv.at[at], {"mem": p})
-
-    def take(p):
-        got = held[block(p), :]
-        for f in range(fields):
-            pick = jnp.where(iota((mloc, rows), 1) == iota((mloc, rows), 0) * fields + f, 1.0, 0.0).astype(BF)
-            lines = nn(pick, got)
-            at = slice(f * cells, (f + 1) * cells)
-            anom[share(p), at] = lines.astype(BF)
-            means[:, at] += jnp.sum(lines, axis=0, keepdims=True)
-
-    def send_block(j, _):
-        block_copy(peer(j), me).start()
-        return 0
-
-    def get_block(j, _):
-        p = source(j)
-        block_copy(p, p).wait_recv()
-        take(p)
-        return 0
-
     def line_of(d):
         k = lax.rem(mz + d, nz)
         return remote(s2.at[cut(k * piece, piece)], r3.at[d], z_send.at[d], z_recv.at[d], {"cell": k})
 
     for d in range(1, nz):
         line_of(d).start()
-    send_block(1, 0)
-    own = pltpu.make_async_copy(x.at[:, col(me)], held.at[block(me)], own_sem)
-    own.start()
-    means[...] = jnp.zeros_like(means)
-    own.wait()
-    take(me)
+    send_block(3, 0)
+    get_block(2, 0)
     acc = s2[cut(mz * piece, piece), :]
     for d in range(1, nz):
         line_of(d).wait_recv()
@@ -250,7 +255,6 @@
 
     for d in range(1, nz):
         line_back(d, mz).start()
-    get_block(1, 0)
     for d in range(1, nz):
         line_back(d, lax.rem(mz + nz - d, nz)).wait_recv()
 
@@ -265,11 +269,12 @@
     for d in range(1, nq):
         plane_back(d, chip).start()
     pair_back(0, core, chip).start()
+    get_block(3, 0)
     for d in range(1, nq):
         q = lax.rem(chip + nq - d, nq)
         plane_back(d, q).wait_recv()
         pair_back(d, core, q).start()
-    lax.fori_loop(2, n, send_block, 0)
+    lax.fori_loop(4, n, send_block, 0)
     for d in range(nq):
         pair_back(d, 1 - core, lax.rem(chip + nq - d, nq)).wait_recv()
 
@@ -373,7 +378,7 @@
         take(q)
         return 0
 
-    lax.fori_loop(1, n // 2, get_two, 0)
+    lax.fori_loop(2, n // 2, get_two, 0)
     means[...] = means[...] / members
 
     def centre(i, _):

time: 97 us -> 95.9 us (0.989)
  no operation moved by 1% of the time
where the time goes in v6:
time: 95.9 us; the launch traced here: 95.7 us
  Pallas kernels  89 us (93%)
  local copies, waits for them, and re-layouts  6.78 us (7%)
    pallas_call x1, Pallas kernels, local(): pl.pallas_call(functools.partial(kernel, dims), out_shape=jax.ShapeDtypeS...  89 us
    reshape x1, local copies, waits for them, and re-layouts, local(): prior_ensemble.reshape(rows, width)  4.14 us
    reshape x1, local copies, waits for them, and re-layouts, local(): return out.reshape(mloc, fields, width)  2.63 us

profile of v6, /device:TPU:0, one launch (start us, length us, event | category | flops | bytes accessed | tf_op | source)
XLA Modules:
  0.0 95.7 jit_solution(15267659747408577845)
XLA Ops:
  0.0 0.0 copy-start.2
  0.0 0.0 copy-start.1
  0.0 0.0 copy-start
  0.0 4.1 %reshape.6.x = bf16[128,8192]{1,0:T(8,128)(2,1)} reshape(bf16[64,2,8192]{2,1,0:T(2,128)(2,1)} %param.4) | data formatting | bytes 4194304 | tf_op jit(solution)/shard_map/reshape | solution.py:504
  4.1 0.0 copy-done.2
  4.1 0.0 copy-done.1
  4.2 0.0 copy-done
  4.2 89.0 %shard_map.46 = bf16[128,8192]{1,0:T(8,128)(2,1)S(1)} custom-call(bf16[128,8192]{1,0:T(8,128)(2,1)} %reshape.6.x, s32[4,128]{1,0:T(4,128)S(1)} %copy-done, f32[4,128]{1,0:T(4,128)S(1)} %copy-done.1, f32[4,128]{1,0:T(4,128)S(1)} %copy-done.2), custom_call_target="tpu_custom_call" | custom-call | tf_op jit(solution)/shard_map/pallas_call | solution.py:495
  93.1 2.6 %reshape.7 = bf16[64,2,8192]{2,1,0:T(2,128)(2,1)} reshape(bf16[128,8192]{1,0:T(8,128)(2,1)S(1)} %shard_map.46) | data formatting | bytes 4194304 | tf_op jit(solution)/shard_map/reshape | solution.py:505
Async XLA Ops:
  0.0 4.1 %copy-start.2 = (f32[4,128]{1,0:T(4,128)S(1)}, f32[4,128]{1,0:T(4,128)}, u32[]{:S(2)}) copy-start(f32[4,128]{1,0:T(4,128)} %spread.1) | copy-start | bytes 6148
  0.0 4.1 %copy-start.1 = (f32[4,128]{1,0:T(4,128)S(1)}, f32[4,128]{1,0:T(4,128)}, u32[]{:S(2)}) copy-start(f32[4,128]{1,0:T(4,128)} %datum.1) | copy-start | bytes 6148
  0.0 4.1 %copy-start = (s32[4,128]{1,0:T(4,128)S(1)}, s32[4,128]{1,0:T(4,128)}, u32[]{:S(2)}) copy-start(s32[4,128]{1,0:T(4,128)} %loc.1) | copy-start | bytes 6148

commit v7 on v6

--- a/solution.py
+++ b/solution.py
@@ -302,7 +302,7 @@
     inv_norm = 1.0 / norm_scale
 
     IP, IU, IQ, IT, IZ = range(5)
-    step = 256 if members % 256 == 0 else LANES
+    step = members
     chunks = members // step
 
     def keep(slot, at, val):
@@ -423,13 +423,16 @@
     def out_copy(p, at):
         return remote(outs.at[p], y.at[:, col(at)], o_send.at[p], o_recv.at[at], {"mem": p})
 
-    def send_out(j, _):
-        p = peer(j)
+    def send_out(i, _):
+        turn = lax.div(i, nq - 1)
+        p = peer(2 * (i - turn * (nq - 1) + 1) + turn)
         outs[p] = make(p)
         out_copy(p, me).start()
         return 0
 
-    lax.fori_loop(1, n, send_out, 0)
+    lax.fori_loop(0, n - 2, send_out, 0)
+    outs[mate] = make(mate)
+    out_copy(mate, me).start()
     outs[me] = make(me)
     own = pltpu.make_async_copy(outs.at[me], y.at[:, col(me)], own_sem)
     own.start()

time: 95.9 us -> 95.3 us (level)
  no operation moved by 1% of the time
where the time goes in v7:
time: 95.3 us; the launch traced here: 95.1 us
  Pallas kernels  88.3 us (93%)
  local copies, waits for them, and re-layouts  6.78 us (7%)
    pallas_call x1, Pallas kernels, local(): pl.pallas_call(functools.partial(kernel, dims), out_shape=jax.ShapeDtypeS...  88.3 us
    reshape x1, local copies, waits for them, and re-layouts, local(): prior_ensemble.reshape(rows, width)  4.14 us
    reshape x1, local copies, waits for them, and re-layouts, local(): return out.reshape(mloc, fields, width)  2.63 us

profile of v7, /device:TPU:0, one launch (start us, length us, event | category | flops | bytes accessed | tf_op | source)
XLA Modules:
  0.0 95.1 jit_solution(3632553167424890834)
XLA Ops:
  0.0 0.0 copy-start.2
  0.0 0.0 copy-start.1
  0.0 0.0 copy-start
  0.0 4.1 %reshape.6.x = bf16[128,8192]{1,0:T(8,128)(2,1)} reshape(bf16[64,2,8192]{2,1,0:T(2,128)(2,1)} %param.4) | data formatting | bytes 4194304 | tf_op jit(solution)/shard_map/reshape | solution.py:507
  4.1 0.0 copy-done.2
  4.1 0.0 copy-done.1
  4.2 0.0 copy-done
  4.2 88.3 %shard_map.46 = bf16[128,8192]{1,0:T(8,128)(2,1)S(1)} custom-call(bf16[128,8192]{1,0:T(8,128)(2,1)} %reshape.6.x, s32[4,128]{1,0:T(4,128)S(1)} %copy-done, f32[4,128]{1,0:T(4,128)S(1)} %copy-done.1, f32[4,128]{1,0:T(4,128)S(1)} %copy-done.2), custom_call_target="tpu_custom_call" | custom-call | tf_op jit(solution)/shard_map/pallas_call | solution.py:498
  92.5 2.6 %reshape.7 = bf16[64,2,8192]{2,1,0:T(2,128)(2,1)} reshape(bf16[128,8192]{1,0:T(8,128)(2,1)S(1)} %shard_map.46) | data formatting | bytes 4194304 | tf_op jit(solution)/shard_map/reshape | solution.py:508
Async XLA Ops:
  0.0 4.1 %copy-start.2 = (f32[4,128]{1,0:T(4,128)S(1)}, f32[4,128]{1,0:T(4,128)}, u32[]{:S(2)}) copy-start(f32[4,128]{1,0:T(4,128)} %spread.1) | copy-start | bytes 6148
  0.0 4.1 %copy-start.1 = (f32[4,128]{1,0:T(4,128)S(1)}, f32[4,128]{1,0:T(4,128)}, u32[]{:S(2)}) copy-start(f32[4,128]{1,0:T(4,128)} %datum.1) | copy-start | bytes 6148
  0.0 4.1 %copy-start = (s32[4,128]{1,0:T(4,128)S(1)}, s32[4,128]{1,0:T(4,128)}, u32[]{:S(2)}) copy-start(s32[4,128]{1,0:T(4,128)} %loc.1) | copy-start | bytes 6148
